TPU v7x, 256 devices: a whole 4x4x8 slice. The times are simulated.
256 devices in a mesh: dp: 16 (over x, y), seq: 16 (over z, core).
Axes of the slice: x: 4, y: 4, z: 8, core: 2. Of those that a mesh axis runs over, the one named last changes fastest.
Arguments:
- queries: bfloat16 [32768, 40, 128], P(('dp', 'seq')), parts along dimension 0, may hold values from -100 to 100
- keys: bfloat16 [32768, 8, 128], P(('dp', 'seq')), parts along dimension 0, may hold values from -4 to 4
- values: bfloat16 [32768, 8, 128], P(('dp', 'seq')), parts along dimension 0, may hold values from -40 to 40
- grad_out: bfloat16 [32768, 40, 128], P(('dp', 'seq')), parts along dimension 0, may hold values from -6 to 6
- doc_ids: int32 [32768], P(('dp', 'seq')), parts along dimension 0, may hold values from 0 to 5, never falling along the last dimension, each value on 1 to 1024 neighbouring positions
Outputs:
- attended: bfloat16 [32768, 40, 128], P(('dp', 'seq')), parts along dimension 0
- grad_queries: bfloat16 [32768, 40, 128], P(('dp', 'seq')), parts along dimension 0
- grad_keys: bfloat16 [32768, 8, 128], P(('dp', 'seq')), parts along dimension 0
- grad_values: bfloat16 [32768, 8, 128], P(('dp', 'seq')), parts along dimension 0
There are 16 independent parts, one for each index of `dp`. A program takes and returns all parts, laid end to end along the dimension named above; each array names one. Nothing has to cross between parts.
Inputs may be any that keep to these rules, and one draw needn't show every extreme that they name: `doc_ids`: document numbers never fall along the sequence, so each document is one contiguous run; the longest runs exactly half of the 2048 positions.
All inputs are finite; a program needn't handle non-finite values.
Results may differ from a plain program's by a relative error of at most 0.04.
Values may be sent and summed in bfloat16 or wider, within the bound.
A program may use at most 192 MiB of HBM per device.

v0:
```python
import math

import jax
import jax.numpy as jnp
import numpy as np
from jax import lax
from jax.sharding import PartitionSpec as P


def as_sent(shard):
    return jax.tree.map(lambda a: a.astype(jnp.bfloat16) if a.dtype == jnp.float32 else a, shard)


def attend(query_rows, query_pos, key_rows, value_rows, grad_rows, doc_all, per_source, local_rows):
    seq_len = key_rows.shape[0]
    query_count = query_rows.shape[0]
    head_size = key_rows.shape[1]
    score_scale = 1.0 / math.sqrt(head_size)
    block_rows = min(512, query_count)
    tile_rows = min(512, seq_len)
    tile_count = seq_len // tile_rows
    key_pos = jnp.arange(seq_len, dtype=jnp.int32)
    key_tiles = [[] for tile_idx in range(tile_count)]
    value_tiles = [[] for tile_idx in range(tile_count)]
    out_parts = []
    query_parts = []
    for first_row in range(0, query_count, block_rows):
        key_limit = min(seq_len, ((first_row + block_rows - 1) // per_source + 1) * local_rows)
        key_limit = min(seq_len, -(-key_limit // tile_rows) * tile_rows)
        q_block = query_rows[first_row : first_row + block_rows]
        g_block = grad_rows[first_row : first_row + block_rows]
        q_where = query_pos[first_row : first_row + block_rows]
        k_block = key_rows[:key_limit]
        v_block = value_rows[:key_limit]
        q_doc = doc_all[q_where]
        k_doc = doc_all[:key_limit]
        allowed = (k_doc[None, :] == q_doc[:, None]) & (
            key_pos[None, :key_limit] <= q_where[:, None]
        )
        scores = (
            jnp.einsum("qd,kd->qk", q_block, k_block, preferred_element_type=jnp.float32)
            * score_scale
        )
        scores = jnp.where(allowed, scores, -jnp.inf)
        row_max = jnp.max(scores, axis=-1, keepdims=True)
        row_sum = jnp.sum(jnp.exp(scores - row_max), axis=-1, keepdims=True)
        probs_low = (jnp.exp(scores - row_max) / row_sum).astype(jnp.bfloat16)
        out_block = jnp.dot(probs_low, v_block, preferred_element_type=jnp.float32).astype(
            jnp.bfloat16
        )
        row_delta = jnp.sum(g_block.astype(jnp.float32) * out_block.astype(jnp.float32), axis=-1)
        grad_prob = jnp.einsum("qd,kd->qk", g_block, v_block, preferred_element_type=jnp.float32)
        grad_score_low = (
            jnp.exp(scores - row_max) / row_sum * (grad_prob - row_delta[:, None])
        ).astype(jnp.bfloat16)
        grad_query = (
            jnp.dot(grad_score_low, k_block, preferred_element_type=jnp.float32) * score_scale
        ).astype(jnp.bfloat16)
        key_part = (
            jnp.einsum("qk,qd->kd", grad_score_low, q_block, preferred_element_type=jnp.float32)
            * score_scale
        )
        value_part = jnp.einsum("qk,qd->kd", probs_low, g_block, preferred_element_type=jnp.float32)
        for tile_idx in range(key_limit // tile_rows):
            key_tiles[tile_idx].append(key_part[tile_idx * tile_rows : (tile_idx + 1) * tile_rows])
            value_tiles[tile_idx].append(
                value_part[tile_idx * tile_rows : (tile_idx + 1) * tile_rows]
            )
        out_parts.append(out_block)
        query_parts.append(grad_query)
    key_sums = []
    value_sums = []
    for tile_idx in range(tile_count):
        key_total = key_tiles[tile_idx][0]
        value_total = value_tiles[tile_idx][0]
        for extra_idx in range(1, len(key_tiles[tile_idx])):
            key_total = key_total + key_tiles[tile_idx][extra_idx]
            value_total = value_total + value_tiles[tile_idx][extra_idx]
        key_sums.append(key_total)
        value_sums.append(value_total)
    key_grad = jnp.concatenate(key_sums, 0)
    value_grad = jnp.concatenate(value_sums, 0)
    return (jnp.concatenate(out_parts, 0), jnp.concatenate(query_parts, 0), key_grad, value_grad)


def to_owners(source, full_heads, seq_size):
    local_rows = source.shape[0]
    head_size = source.shape[2]
    main_part = source[:, : full_heads * seq_size].reshape(
        local_rows, seq_size, full_heads, head_size
    )
    main_part = jnp.transpose(main_part, (1, 2, 0, 3)).reshape(
        seq_size, full_heads * local_rows, head_size
    )
    extra = source[:, full_heads * seq_size :]
    if extra.shape[1] == 0:
        return main_part
    odd_count = extra.shape[1]
    extra_part = extra.reshape(2, local_rows // 2, odd_count, head_size)
    extra_part = jnp.transpose(extra_part, (2, 0, 1, 3)).reshape(
        seq_size, local_rows // 2, head_size
    )
    return jnp.concatenate([main_part, extra_part], axis=1)


def from_owners(received, full_heads, odd_heads, seq_size, local_rows):
    head_size = received.shape[2]
    main_part = received[:, : full_heads * local_rows].reshape(
        seq_size, full_heads, local_rows, head_size
    )
    main_part = jnp.transpose(main_part, (2, 0, 1, 3)).reshape(
        local_rows, seq_size * full_heads, head_size
    )
    extra = received[:, full_heads * local_rows :]
    extra_part = extra.reshape(odd_heads, 2, local_rows // 2, head_size)
    extra_part = jnp.transpose(extra_part, (1, 2, 0, 3)).reshape(local_rows, odd_heads, head_size)
    return jnp.concatenate([main_part, extra_part], axis=1)


def shards(queries, keys, values, grad_out, doc_ids):
    local_rows = queries.shape[0]
    head_size = queries.shape[2]
    q_heads = queries.shape[1]
    kv_heads = keys.shape[1]
    group_size = q_heads // kv_heads
    seq_size = lax.axis_size("seq")
    device = lax.axis_index("seq")
    full_heads = q_heads // seq_size
    odd_heads = q_heads % seq_size
    slot_count = full_heads + 1
    seq_len = local_rows * seq_size
    half_rows = local_rows // 2
    row_offset = device % 2 * half_rows
    dev_range = np.arange(seq_size)
    full_table = dev_range[:, None] * full_heads + np.arange(full_heads)[None, :]
    odd_list = full_heads * seq_size + np.arange(odd_heads)
    head_order = np.concatenate([full_table.reshape(-1), odd_list]).astype(np.int32)
    reordered = not bool(np.all(head_order == np.arange(q_heads)))
    inverse_order = np.argsort(head_order).astype(np.int32)
    head_table = np.concatenate([full_table, odd_list[dev_range // 2][:, None]], axis=1)
    kv_table = (head_table // group_size).astype(np.int32)
    single_group = bool(np.all(kv_table == kv_table[:, :1]))
    if reordered:
        queries_in = jnp.take(queries, head_order, axis=1)
        grad_in = jnp.take(grad_out, head_order, axis=1)
    else:
        queries_in = queries
        grad_in = grad_out
    if single_group:
        kv_column = kv_table[:, 0]

        def kv_to_owners(source):
            picked = jnp.take(source, kv_column, axis=1)
            return jnp.transpose(picked, (1, 0, 2))

    else:

        def kv_to_owners(source):
            picked = jnp.take(source, kv_table.reshape(-1), axis=1).reshape(
                local_rows, seq_size, slot_count, head_size
            )
            return jnp.transpose(picked, (1, 2, 0, 3)).reshape(
                seq_size, slot_count * local_rows, head_size
            )

    q_send = to_owners(queries_in, full_heads, seq_size)
    g_send = to_owners(grad_in, full_heads, seq_size)
    k_send = kv_to_owners(keys)
    v_send = kv_to_owners(values)
    q_recv, k_recv, v_recv, g_recv = (
        lax.all_to_all(q_send, "seq", split_axis=0, concat_axis=0, tiled=True),
        lax.all_to_all(as_sent(k_send), "seq", split_axis=0, concat_axis=0, tiled=True).astype(
            k_send.dtype
        ),
        lax.all_to_all(as_sent(v_send), "seq", split_axis=0, concat_axis=0, tiled=True).astype(
            v_send.dtype
        ),
        lax.all_to_all(g_send, "seq", split_axis=0, concat_axis=0, tiled=True),
    )
    doc_all = lax.all_gather(doc_ids, "seq", axis=0, tiled=True)
    full_pos = jnp.arange(seq_len, dtype=jnp.int32)
    odd_pos = (
        jnp.arange(seq_size, dtype=jnp.int32)[:, None] * local_rows
        + row_offset
        + jnp.arange(half_rows, dtype=jnp.int32)[None, :]
    ).reshape(-1)
    out_slots = []
    query_slots = []
    key_slots = []
    value_slots = []
    for slot_idx in range(slot_count):
        if single_group:
            k_slot = k_recv.reshape(seq_len, head_size)
            v_slot = v_recv.reshape(seq_len, head_size)
        else:
            k_slot = k_recv[:, slot_idx * local_rows : (slot_idx + 1) * local_rows].reshape(
                seq_len, head_size
            )
            v_slot = v_recv[:, slot_idx * local_rows : (slot_idx + 1) * local_rows].reshape(
                seq_len, head_size
            )
        if slot_idx < full_heads:
            q_slot = q_recv[:, slot_idx * local_rows : (slot_idx + 1) * local_rows].reshape(
                seq_len, head_size
            )
            g_slot = g_recv[:, slot_idx * local_rows : (slot_idx + 1) * local_rows].reshape(
                seq_len, head_size
            )
            slot_pos = full_pos
            per_source = local_rows
        else:
            q_slot = q_recv[:, full_heads * local_rows :].reshape(-1, head_size)
            g_slot = g_recv[:, full_heads * local_rows :].reshape(-1, head_size)
            slot_pos = odd_pos
            per_source = half_rows
        out_rows, query_grad, key_grad, value_grad = attend(
            q_slot, slot_pos, k_slot, v_slot, g_slot, doc_all, per_source, local_rows
        )
        out_slots.append(out_rows.reshape(seq_size, per_source, head_size))
        query_slots.append(query_grad.reshape(seq_size, per_source, head_size))
        key_slots.append(key_grad.reshape(seq_size, local_rows, head_size))
        value_slots.append(value_grad.reshape(seq_size, local_rows, head_size))
    out_send = jnp.concatenate(out_slots, axis=1)
    dq_send = jnp.concatenate(query_slots, axis=1)
    out_recv, dq_recv = (
        lax.all_to_all(as_sent(out_send), "seq", split_axis=0, concat_axis=0, tiled=True).astype(
            out_send.dtype
        ),
        lax.all_to_all(as_sent(dq_send), "seq", split_axis=0, concat_axis=0, tiled=True).astype(
            dq_send.dtype
        ),
    )
    attended = from_owners(out_recv, full_heads, odd_heads, seq_size, local_rows)
    grad_queries = from_owners(dq_recv, full_heads, odd_heads, seq_size, local_rows)
    if reordered:
        attended = jnp.take(attended, inverse_order, axis=1)
        grad_queries = jnp.take(grad_queries, inverse_order, axis=1)
    if single_group:
        dk_send = key_slots[0]
        dv_send = value_slots[0]
        for slot_idx in range(1, slot_count):
            dk_send = dk_send + key_slots[slot_idx]
            dv_send = dv_send + value_slots[slot_idx]
    else:
        dk_send = jnp.stack(key_slots, axis=1).reshape(seq_size, slot_count * local_rows, head_size)
        dv_send = jnp.stack(value_slots, axis=1).reshape(
            seq_size, slot_count * local_rows, head_size
        )
    dk_recv, dv_recv = (
        lax.all_to_all(dk_send, "seq", split_axis=0, concat_axis=0, tiled=True),
        lax.all_to_all(dv_send, "seq", split_axis=0, concat_axis=0, tiled=True),
    )
    if single_group:
        source_hot = (kv_column[:, None] == np.arange(kv_heads)[None, :]).astype(np.float32)
        grad_keys = jnp.einsum(
            "dlh,dg->lgh", dk_recv, source_hot, precision=lax.Precision.HIGHEST
        ).astype(jnp.bfloat16)
        grad_values = jnp.einsum(
            "dlh,dg->lgh", dv_recv, source_hot, precision=lax.Precision.HIGHEST
        ).astype(jnp.bfloat16)
    else:
        one_hot = (kv_table[:, :, None] == np.arange(kv_heads)[None, None, :]).astype(np.float32)
        grad_keys = jnp.einsum(
            "dslh,dsg->lgh",
            dk_recv.reshape(seq_size, slot_count, local_rows, head_size),
            one_hot,
            precision=lax.Precision.HIGHEST,
        ).astype(jnp.bfloat16)
        grad_values = jnp.einsum(
            "dslh,dsg->lgh",
            dv_recv.reshape(seq_size, slot_count, local_rows, head_size),
            one_hot,
            precision=lax.Precision.HIGHEST,
        ).astype(jnp.bfloat16)
    return (attended, grad_queries, grad_keys, grad_values)


def solution(mesh):
    return jax.shard_map(
        shards,
        mesh=mesh,
        in_specs=(
            P(("dp", "seq"), None, None),
            P(("dp", "seq"), None, None),
            P(("dp", "seq"), None, None),
            P(("dp", "seq"), None, None),
            P(("dp", "seq")),
        ),
        out_specs=(
            P(("dp", "seq"), None, None),
            P(("dp", "seq"), None, None),
            P(("dp", "seq"), None, None),
            P(("dp", "seq"), None, None),
        ),
        check_vma=False,
    )
```

profile of v0, /device:TPU:12, one launch (start us, length us, event | category | flops | bytes accessed | tf_op | source)
XLA Modules:
  0.0 495.9 jit_solution(8859444619226739147)
XLA Ops:
  2.5 1.2 pad_maximum_fusion.2
  3.6 8.7 %all-to-all-start = ((bf16[16,320,128]{2,1,0:T(8,128)(2,1)}), bf16[16,320,128]{2,1,0:T(8,128)(2,1)S(1)}, u32[]{:S(2)}, u32[]{:S(2)}) async-start(bf16[16,320,128]{2,1,0:T(8,128)(2,1)} %pad_maximum_fusion.2), calls=%async_computation | async-start | bytes 2621440 | tf_op jit(solution)/shard_map/all_to_all | solution.py:171
  12.4 1.2 slice-done.3
  14.0 1.2 pad_maximum_fusion.5
  15.1 29.4 %all-to-all-done = bf16[16,320,128]{2,1,0:T(8,128)(2,1)S(1)} async-done(((bf16[16,320,128]{2,1,0:T(8,128)(2,1)}), bf16[16,320,128]{2,1,0:T(8,128)(2,1)S(1)}, u32[]{:S(2)}, u32[]{:S(2)}) %all-to-all-start) | async-done | bytes 1310752 | tf_op jit(solution)/shard_map/all_to_all | solution.py:171
  44.5 4.9 all-to-all-start.4
  49.4 8.6 %gather_fusion.6 = bf16[48,128,128]{2,0,1:T(8,128)(2,1)S(1)} fusion(bf16[128,8,128]{2,1,0:T(8,128)(2,1)S(1)} %copy-done, s32[1024]{0:T(1024)S(1)} %pad_clamp_fusion.5), kind=kCustom, calls=%fused_computation.clone | custom fusion | bytes 3145920 | tf_op jit(solution)/shard_map/jit(_take)/gather | solution.py:159
  58.1 1.6 copy.43
  59.7 21.9 %all-to-all-done.4 = bf16[16,320,128]{2,1,0:T(8,128)(2,1)S(1)} async-done(((bf16[16,320,128]{2,1,0:T(8,128)(2,1)}), bf16[16,320,128]{2,1,0:T(8,128)(2,1)S(1)}, u32[]{:S(2)}, u32[]{:S(2)}) %all-to-all-start.4) | async-done | bytes 1310752 | tf_op jit(solution)/shard_map/all_to_all | solution.py:178
  81.6 5.0 %all-to-all-start.1 = ((bf16[16,384,128]{2,1,0:T(8,128)(2,1)}), bf16[16,384,128]{2,1,0:T(8,128)(2,1)S(1)}, u32[]{:S(2)}, u32[]{:S(2)}) async-start(bf16[16,384,128]{2,1,0:T(8,128)(2,1)} %bitcast.13), calls=%async_computation.1 | async-start | bytes 3145728 | tf_op jit(solution)/shard_map/all_to_all | solution.py:172
  86.9 8.6 %gather_fusion.7 = bf16[48,128,128]{2,0,1:T(8,128)(2,1)S(1)} fusion(bf16[128,8,128]{2,1,0:T(8,128)(2,1)S(1)} %copy-done.2, s32[1024]{0:T(1024)S(1)} %pad_clamp_fusion.5), kind=kCustom, calls=%fused_computation.1.clone | custom fusion | bytes 3145920 | tf_op jit(solution)/shard_map/jit(_take)/gather | solution.py:159
  95.5 1.6 copy.44
  97.3 27.2 %all-to-all-done.1 = bf16[16,384,128]{2,1,0:T(8,128)(2,1)S(1)} async-done(((bf16[16,384,128]{2,1,0:T(8,128)(2,1)}), bf16[16,384,128]{2,1,0:T(8,128)(2,1)S(1)}, u32[]{:S(2)}, u32[]{:S(2)}) %all-to-all-start.1) | async-done | bytes 1572896 | tf_op jit(solution)/shard_map/all_to_all | solution.py:172
  124.5 4.9 all-to-all-start.2
  129.5 48.0 %all-gather = s32[16,1,128]{2,1,0:T(1,128)S(1)} all-gather(s32[1,1,128]{2,1,0:T(1,128)S(1)} %bitcast.385), channel_id=1, replica_groups=mesh['dp'=16,'seq'=16] {'seq'}, dimensions={0}, use_global_device_ids=true | all-gather | bytes 8704 | tf_op jit(solution)/shard_map/all_gather | solution.py:180
  177.5 3.1 gather_fusion.2
  180.7 3.1 gather_fusion.3
  183.8 3.1 gather_fusion.1
  187.0 3.1 gather_fusion
  190.1 3.1 gather_fusion.4
  193.3 3.4 gather_fusion.5
  196.7 1.7 fusion.113
  198.4 1.7 fusion.111
  200.2 2.3 fusion.112
  203.4 1.1 fusion.108
  204.5 1.2 fusion.115
  206.4 2.7 fusion.6
  210.2 3.1 multiply_reduce_fusion
  214.7 1.4 fusion.66
  216.1 1.7 convolution_multiply_fusion.4
  227.6 1.1 fusion.71
  232.2 1.1 fusion.69
  236.4 1.1 fusion.70
  241.8 1.2 fusion.68
  246.8 1.2 fusion.67
  248.4 1.4 fusion.121
  252.3 1.2 copy-done.6
  254.2 1.4 fusion.63
  255.8 1.2 fusion.117
  259.5 1.2 copy-done.4
  260.8 1.2 pad_maximum_fusion.3
  261.9 6.1 %all-to-all-start.3 = ((bf16[16,320,128]{2,1,0:T(8,128)(2,1)}), bf16[16,320,128]{2,1,0:T(8,128)(2,1)}, u32[]{:S(2)}, u32[]{:S(2)}) async-start(bf16[16,320,128]{2,1,0:T(8,128)(2,1)} %pad_maximum_fusion.3), calls=%async_computation.3 | async-start | bytes 2621440 | tf_op jit(solution)/shard_map/all_to_all | solution.py:226
  268.1 3.2 multiply_convert_fusion.1
  274.1 1.1 pad_maximum_fusion.6
  281.6 18.7 %all-to-all-done.3 = bf16[16,320,128]{2,1,0:T(8,128)(2,1)} async-done(((bf16[16,320,128]{2,1,0:T(8,128)(2,1)}), bf16[16,320,128]{2,1,0:T(8,128)(2,1)}, u32[]{:S(2)}, u32[]{:S(2)}) %all-to-all-start.3) | async-done | bytes 1310752 | tf_op jit(solution)/shard_map/all_to_all | solution.py:226
  300.3 4.9 all-to-all-start.5
  305.3 1.4 pad_maximum_fusion.10
  306.8 1.5 fusion.61
  312.6 1.9 pad_maximum_fusion
  314.5 23.0 %all-to-all-done.5 = bf16[16,320,128]{2,1,0:T(8,128)(2,1)} async-done(((bf16[16,320,128]{2,1,0:T(8,128)(2,1)}), bf16[16,320,128]{2,1,0:T(8,128)(2,1)}, u32[]{:S(2)}, u32[]{:S(2)}) %all-to-all-start.5) | async-done | bytes 1310752 | tf_op jit(solution)/shard_map/all_to_all | solution.py:229
  337.5 5.2 %all-to-all-start.6 = ((f32[16,384,128]{2,1,0:T(8,128)}), f32[16,384,128]{2,1,0:T(8,128)}, u32[]{:S(2)}, u32[]{:S(2)}) async-start(f32[16,384,128]{2,1,0:T(8,128)} %bitcast.265), calls=%async_computation.6 | async-start | bytes 6291456 | tf_op jit(solution)/shard_map/all_to_all | solution.py:250
  342.7 3.1 fusion.72
  346.5 1.4 copy-done.15
  352.5 1.2 copy-done.13
  354.8 1.1 copy-done.5
  358.2 1.9 pad_maximum_fusion.1
  360.1 54.4 %all-to-all-done.6 = f32[16,384,128]{2,1,0:T(8,128)} async-done(((f32[16,384,128]{2,1,0:T(8,128)}), f32[16,384,128]{2,1,0:T(8,128)}, u32[]{:S(2)}, u32[]{:S(2)}) %all-to-all-start.6) | async-done | bytes 3145760 | tf_op jit(solution)/shard_map/all_to_all | solution.py:250
  414.5 5.0 %all-to-all-start.7 = ((f32[16,384,128]{2,1,0:T(8,128)}), f32[16,384,128]{2,1,0:T(8,128)S(1)}, u32[]{:S(2)}, u32[]{:S(2)}) async-start(f32[16,384,128]{2,1,0:T(8,128)} %bitcast.102), calls=%async_computation.7 | async-start | bytes 6291456 | tf_op jit(solution)/shard_map/all_to_all | solution.py:251
  419.5 1.3 slice.685
  423.0 1.3 slice.697
  426.6 1.9 pad_maximum_fusion.4
  428.6 6.0 %fusion.46 = bf16[128,8,128]{2,1,0:T(8,128)(2,1)} fusion(f32[16,3,8,1]{0,2,1,3:T(8,128)S(1)} %copy-done.100, f32[16,3,128,128]{3,2,1,0:T(8,128)} %bitcast.91), kind=kOutput, calls=%fused_computation.94 | convolution fusion | flops 75628544 | bytes 3409408 | tf_op jit(solution)/shard_map/dslh,dsg->lgh/dot_general | solution.py:263
  434.6 56.6 %all-to-all-done.7 = f32[16,384,128]{2,1,0:T(8,128)S(1)} async-done(((f32[16,384,128]{2,1,0:T(8,128)}), f32[16,384,128]{2,1,0:T(8,128)S(1)}, u32[]{:S(2)}, u32[]{:S(2)}) %all-to-all-start.7) | async-done | bytes 3145760 | tf_op jit(solution)/shard_map/all_to_all | solution.py:251
  491.2 4.2 fusion.49
  (339 shorter events, 63.2 us)
Async XLA Ops:
  0.6 48.8 %copy-start = (bf16[128,8,128]{2,1,0:T(8,128)(2,1)S(1)}, bf16[128,8,128]{2,1,0:T(8,128)(2,1)}, u32[]{:S(2)}) copy-start(bf16[128,8,128]{2,1,0:T(8,128)(2,1)} %param.12) | copy-start | bytes 786436
  3.6 8.7 %slice-start.2 = ((bf16[128,40,128]{2,1,0:T(8,128)(2,1)}), bf16[128,8,128]{2,1,0:T(8,128)(2,1)S(1)}, s32[]{:S(2)}) async-start(bf16[128,40,128]{2,1,0:T(8,128)(2,1)} %param.14), calls=%async_computation.10 | async-start | bytes 524288 | tf_op jit(solution)/shard_map/slice | solution.py:95
  3.6 40.9 %all-to-all-start = ((bf16[16,320,128]{2,1,0:T(8,128)(2,1)}), bf16[16,320,128]{2,1,0:T(8,128)(2,1)S(1)}, u32[]{:S(2)}, u32[]{:S(2)}) async-start(bf16[16,320,128]{2,1,0:T(8,128)(2,1)} %pad_maximum_fusion.2), calls=%async_computation | async-start | bytes 2621440 | tf_op jit(solution)/shard_map/all_to_all | solution.py:171
  14.0 35.5 %copy-start.102 = (s32[48]{0:T(128)S(1)}, s32[48]{0:T(128)}, u32[]{:S(2)}) copy-start(s32[48]{0:T(128)} %constant.76) | copy-start | bytes 580
  44.5 4.9 copy-start.34
  44.5 37.1 %all-to-all-start.4 = ((bf16[16,320,128]{2,1,0:T(8,128)(2,1)}), bf16[16,320,128]{2,1,0:T(8,128)(2,1)S(1)}, u32[]{:S(2)}, u32[]{:S(2)}) async-start(bf16[16,320,128]{2,1,0:T(8,128)(2,1)} %pad_maximum_fusion.5), calls=%async_computation.4 | async-start | bytes 2621440 | tf_op jit(solution)/shard_map/all_to_all | solution.py:178
  59.7 27.2 %copy-start.2 = (bf16[128,8,128]{2,1,0:T(8,128)(2,1)S(1)}, bf16[128,8,128]{2,1,0:T(8,128)(2,1)}, u32[]{:S(2)}) copy-start(bf16[128,8,128]{2,1,0:T(8,128)(2,1)} %param.13) | copy-start | bytes 786436
  81.6 5.2 %copy-start.35 = (bf16[16,320,128]{2,1,0:T(8,128)(2,1)}, bf16[16,320,128]{2,1,0:T(8,128)(2,1)S(1)}, u32[]{:S(2)}) copy-start(bf16[16,320,128]{2,1,0:T(8,128)(2,1)S(1)} %all-to-all-done.4) | copy-start | bytes 3932164
  81.6 42.9 %all-to-all-start.1 = ((bf16[16,384,128]{2,1,0:T(8,128)(2,1)}), bf16[16,384,128]{2,1,0:T(8,128)(2,1)S(1)}, u32[]{:S(2)}, u32[]{:S(2)}) async-start(bf16[16,384,128]{2,1,0:T(8,128)(2,1)} %bitcast.13), calls=%async_computation.1 | async-start | bytes 3145728 | tf_op jit(solution)/shard_map/all_to_all | solution.py:172
  97.1 32.4 %copy-start.101 = (s32[128]{0:T(128)S(1)}, s32[128]{0:T(128)}, u32[]{:S(2)}) copy-start(s32[128]{0:T(128)} %param.15) | copy-start | bytes 1540
  124.5 84.7 %all-to-all-start.2 = ((bf16[16,384,128]{2,1,0:T(8,128)(2,1)}), bf16[16,384,128]{2,1,0:T(8,128)(2,1)S(1)}, u32[]{:S(2)}, u32[]{:S(2)}) async-start(bf16[16,384,128]{2,1,0:T(8,128)(2,1)} %bitcast.267), calls=%async_computation.2 | async-start | bytes 3145728 | tf_op jit(solution)/shard_map/all_to_all | solution.py:175
  196.6 5.8 %copy-start.36 = (bf16[16,320,128]{2,1,0:T(8,128)(2,1)S(1)}, bf16[16,320,128]{2,1,0:T(8,128)(2,1)}, u32[]{:S(2)}) copy-start(bf16[16,320,128]{2,1,0:T(8,128)(2,1)} %copy-done.35) | copy-start | bytes 3932164
  198.4 6.1 %copy-start.75 = (bf16[8,64,128]{2,1,0:T(8,128)(2,1)}, bf16[8,64,128]{2,1,0:T(8,128)(2,1)S(1)}, u32[]{:S(2)}) copy-start(bf16[8,64,128]{2,1,0:T(8,128)(2,1)S(1)} %get-tuple-element.56) | copy-start | bytes 393220
  209.2 16.6 %copy-start.20 = (bf16[16,384,128]{2,1,0:T(8,128)(2,1)}, bf16[16,384,128]{2,1,0:T(8,128)(2,1)S(1)}, u32[]{:S(2)}) copy-start(bf16[16,384,128]{2,1,0:T(8,128)(2,1)S(1)} %all-to-all-done.2) | copy-start | bytes 4718596
  209.3 49.4 %copy-start.41 = (bf16[16,128,128]{2,1,0:T(8,128)(2,1)}, bf16[16,128,128]{2,1,0:T(8,128)(2,1)S(1)}, u32[]{:S(2)}) copy-start(bf16[16,128,128]{2,1,0:T(8,128)(2,1)S(1)} %get-tuple-element.36) | copy-start | bytes 1572868
  210.2 3.4 copy-start.3
  216.1 1.7 copy-start.82
  227.6 2.2 copy-start.28
  232.2 1.8 copy-start.30
  236.4 2.1 copy-start.26
  241.8 2.1 copy-start.22
  245.2 1.6 copy-start.8
  246.8 3.1 copy-start.24
  246.8 1.6 copy-start.79
  251.4 2.1 copy-start.6
  254.2 2.9 copy-start.16
  254.2 1.6 copy-start.77
  258.7 2.0 copy-start.4
  261.9 38.4 %all-to-all-start.3 = ((bf16[16,320,128]{2,1,0:T(8,128)(2,1)}), bf16[16,320,128]{2,1,0:T(8,128)(2,1)}, u32[]{:S(2)}, u32[]{:S(2)}) async-start(bf16[16,320,128]{2,1,0:T(8,128)(2,1)} %pad_maximum_fusion.3), calls=%async_computation.3 | async-start | bytes 2621440 | tf_op jit(solution)/shard_map/all_to_all | solution.py:226
  268.1 3.3 copy-start.90
  268.1 3.3 copy-start.94
  268.1 3.3 copy-start.96
  268.1 3.3 copy-start.99
  268.1 3.4 copy-start.32
  271.4 2.6 copy-start.18
  271.4 1.8 copy-start.78
  271.5 2.5 copy-start.89
  271.5 2.5 copy-start.93
  271.5 2.5 copy-start.97
  274.0 1.7 copy-start.92
  275.7 2.0 copy-start.25
  275.7 2.0 copy-start.74
  277.0 1.7 copy-start.17
  277.0 1.7 copy-start.72
  277.6 1.8 copy-start.47
  300.3 37.1 %all-to-all-start.5 = ((bf16[16,320,128]{2,1,0:T(8,128)(2,1)}), bf16[16,320,128]{2,1,0:T(8,128)(2,1)}, u32[]{:S(2)}, u32[]{:S(2)}) async-start(bf16[16,320,128]{2,1,0:T(8,128)(2,1)} %pad_maximum_fusion.6), calls=%async_computation.5 | async-start | bytes 2621440 | tf_op jit(solution)/shard_map/all_to_all | solution.py:229
  305.3 3.0 copy-start.64
  305.3 3.0 copy-start.65
  305.3 3.0 copy-start.66
  306.7 1.6 copy-start.27
  306.8 1.6 copy-start.85
  308.4 2.0 copy-start.19
  308.4 2.0 copy-start.68
  337.5 77.0 %all-to-all-start.6 = ((f32[16,384,128]{2,1,0:T(8,128)}), f32[16,384,128]{2,1,0:T(8,128)}, u32[]{:S(2)}, u32[]{:S(2)}) async-start(f32[16,384,128]{2,1,0:T(8,128)} %bitcast.265), calls=%async_computation.6 | async-start | bytes 6291456 | tf_op jit(solution)/shard_map/all_to_all | solution.py:250
  342.7 3.1 copy-start.11
  342.7 3.1 copy-start.54
  346.3 1.6 copy-start.15
  346.4 2.5 copy-start.9
  347.9 2.4 copy-start.7
  353.7 2.2 copy-start.5
  354.2 1.8 copy-start.56
  414.5 76.8 %all-to-all-start.7 = ((f32[16,384,128]{2,1,0:T(8,128)}), f32[16,384,128]{2,1,0:T(8,128)S(1)}, u32[]{:S(2)}, u32[]{:S(2)}) async-start(f32[16,384,128]{2,1,0:T(8,128)} %bitcast.102), calls=%async_computation.7 | async-start | bytes 6291456 | tf_op jit(solution)/shard_map/all_to_all | solution.py:251
  426.6 2.0 copy-start.100
  428.6 66.9 %copy-start.1 = (bf16[128,8,128]{2,1,0:T(8,128)(2,1)S(1)}, bf16[128,8,128]{2,1,0:T(8,128)(2,1)}, u32[]{:S(2)}) copy-start(bf16[128,8,128]{2,1,0:T(8,128)(2,1)} %param.12) | copy-start | bytes 786436
  (51 other events, 61.2 us)
where the time goes:
time: 505 us; the launch traced here: 496 us
  waiting for transfers between devices  231 us (46%)
  local copies, waits for them, and re-layouts  80 us (16%)
  matrix products  62 us (12%)
  blocking collectives  48 us (10%)
  starting transfers between devices  44.8 us (9%)
  other arithmetic  27.2 us (5%)
    all_to_all x1, waiting for transfers between devices, shards(): lax.all_to_all(dv_send, 'seq', split_axis=0, concat_axis=0, tiled=True)  56.6 us
    all_to_all x1, waiting for transfers between devices, shards(): lax.all_to_all(dk_send, 'seq', split_axis=0, concat_axis=0, tiled=True)  54.4 us
    all_gather x1, blocking collectives, shards(): doc_all = lax.all_gather(doc_ids, 'seq', axis=0, tiled=True)  48 us
    all_to_all x1, waiting for transfers between devices, shards(): lax.all_to_all(q_send, 'seq', split_axis=0, concat_axis=0, tiled=True)  29.4 us
    all_to_all x1, waiting for transfers between devices, shards(): lax.all_to_all(as_sent(k_send), 'seq', split_axis=0, concat_axis=0, tiled...  27.2 us
    all_to_all x1, waiting for transfers between devices, shards(): lax.all_to_all(as_sent(dq_send), 'seq', split_axis=0, concat_axis=0, tile...  23 us
    all_to_all x1, waiting for transfers between devices, shards(): lax.all_to_all(g_send, 'seq', split_axis=0, concat_axis=0, tiled=True)  21.9 us
    unnamed x206, local copies, waits for them, and re-layouts  20.5 us
  transfers between devices with their start and end apart: 8, of which 7 were waited for; matrix products, arithmetic and copies ran while one was open for 19% of the time, Pallas kernels for 0%

commit v1 on v0

v1 whole, which is shorter than its diff:
```python
import functools
import math

import jax
import jax.numpy as jnp
from jax import lax
from jax.experimental import pallas as pl
from jax.experimental.pallas import tpu as pltpu
from jax.sharding import PartitionSpec as P

MESH = pl.DeviceIdType.MESH
COMPUTE = True
COMM = True
BACK = 4
LINE = BACK + 1
DOC_VALUES = 6


def rows_at(distance, rows):
    return pl.ds(pl.multiple_of((2 * BACK - distance) * rows, rows), rows)


def kernel(
    q_ref, g_ref, kv_ref, doc_ref, o_ref, dq_ref, dkv_ref,
    kv_all, doc_all, part_own, part_sib, sib_got, sums, sums_got,
    s_ref, p_ref, ds_ref, qt_ref, gt_ref, qs_ref, gs_ref, kt_ref, vt_ref,
    start_ref, delta_ref, inv_ref,
    kv_up_recv, kv_sib_recv, doc_up_recv, doc_sib_recv, sib_recv, sums_recv,
    send_sems,
):
    units, rows, head = kv_ref.shape
    groups = units // 2
    cols = q_ref.shape[1]
    members = cols // rows
    window = kv_all.shape[1]
    blocks = window // rows
    size = lax.axis_size("seq")
    me = lax.axis_index("seq")
    core = lax.rem(me, 2)
    up = lax.rem(me + 2, size)
    down = lax.rem(me + size - 2, size)
    sib = me + 1 - 2 * core
    scale = 1.0 / math.sqrt(head)
    log_scale = scale * math.log2(math.e)
    f32, bf16 = jnp.float32, jnp.bfloat16

    own = pl.ds(window - rows, rows)
    kv_all[:, own, :] = kv_ref[...]
    doc_all[64:72, :] = doc_ref[...]
    sib_got[:, 0] = jnp.zeros((units, rows, head), bf16)
    sib_got[:, BACK] = jnp.zeros((units, rows, head), bf16)

    def remote(src, dst, send, recv, to):
        return pltpu.make_async_remote_copy(
            src_ref=src, dst_ref=dst, send_sem=send_sems.at[send], recv_sem=recv,
            device_id={"seq": to}, device_id_type=MESH,
        )

    def kv_up(unit, k):
        return remote(
            kv_all.at[unit, rows_at(2 * k, rows)], kv_all.at[unit, rows_at(2 * k + 2, rows)],
            0, kv_up_recv.at[unit, k], up,
        )

    def kv_share(unit, k):
        slot = k - core
        return remote(
            kv_all.at[unit, rows_at(2 * k, rows)], kv_all.at[unit, rows_at(2 * slot + 1, rows)],
            1, kv_sib_recv.at[unit, slot], sib,
        )

    def doc_up(k):
        return remote(
            doc_all.at[rows_at(2 * k, 8)], doc_all.at[rows_at(2 * k + 2, 8)],
            2, doc_up_recv.at[k], up,
        )

    def doc_share(k):
        slot = k - core
        return remote(
            doc_all.at[rows_at(2 * k, 8)], doc_all.at[rows_at(2 * slot + 1, 8)],
            3, doc_sib_recv.at[slot], sib,
        )

    def part_share(unit):
        return remote(
            part_sib.at[unit], sib_got.at[unit, pl.ds(1 - core, BACK)],
            4, sib_recv.at[unit], sib,
        )

    def sum_down(unit, j):
        return remote(
            sums.at[unit, j - 1], sums_got.at[unit, j - 1],
            5, sums_recv.at[unit, j - 1], down,
        )

    barrier = pltpu.get_barrier_semaphore()
    for other in (up, down, sib):
        pl.semaphore_signal(barrier, inc=1, device_id={"seq": other}, device_id_type=MESH)
    pl.semaphore_wait(barrier, 3)

    def kv_event(step, k):
        unit = step - k

        @pl.when((unit >= 0) & (unit < units))
        def _():
            if k > 0:
                @pl.when(unit == 0)
                def _():
                    doc_up(k - 1).wait_recv()
                kv_up(unit, k - 1).wait_recv()
            if k < BACK:
                @pl.when(unit == 0)
                def _():
                    doc_up(k).start()
                kv_up(unit, k).start()

            def share():
                @pl.when(unit == 0)
                def _():
                    doc_share(k).start()
                kv_share(unit, k).start()

            if k == 0:
                pl.when(core == 0)(share)
            elif k == BACK:
                pl.when(core == 1)(share)
            else:
                share()

    def sum_event(step, j):
        unit = step - 2 * BACK + 1 - (BACK - j)

        @pl.when((unit >= 0) & (unit < units))
        def _():
            if j == BACK:
                part_share(unit).wait_recv()
            total = part_own[unit, j] + sib_got[unit, j].astype(f32)
            if j < BACK:
                sum_down(unit, j + 1).wait_recv()
                total = total + sums_got[unit, j].astype(f32)
            if j > 0:
                sums[unit, j - 1] = total.astype(bf16)
                sum_down(unit, j).start()
            else:
                factor = jnp.where(unit % 2 == 1, scale, 1.0).astype(f32)
                dkv_ref[unit] = (total * factor).astype(bf16)

    def find_starts():
        docs = doc_ref[0:1, :]
        old = lax.broadcasted_iota(jnp.int32, (8 * blocks, rows), 0) // 8
        old = old + (me - 2 * BACK) < 0
        all_docs = jnp.where(old, -1, doc_all[...])
        start = jnp.zeros((1, rows), jnp.int32)
        for value in range(DOC_VALUES):
            less = jnp.where(all_docs < value, 1, 0)
            count = jnp.sum(jnp.sum(less, axis=0, keepdims=True), axis=1, keepdims=True) // 8
            start = jnp.where(docs == value, count, start)
        for member in range(members):
            start_ref[:, member * rows : (member + 1) * rows] = start

    def forward(group, first, width):
        at = slice(first, first + width)
        qt = q_ref[group, at, :].T
        qt_ref[:, at] = qt
        start = start_ref[:, at]
        top = jnp.full((8, width), -jnp.inf, f32)
        for block in range(blocks):
            span = slice(block * rows, (block + 1) * rows)
            s = jnp.dot(kv_all[2 * group, span, :], qt, preferred_element_type=f32)
            where = block * rows + lax.broadcasted_iota(jnp.int32, (rows, width), 0)
            allowed = where >= start
            if block == blocks - 1:
                mine = lax.broadcasted_iota(jnp.int32, (rows, width), 1) % rows
                allowed = allowed & (where - block * rows <= mine)
            s = jnp.where(allowed, s, -jnp.inf)
            s_ref[span, at] = s
            top = jnp.maximum(top, jnp.max(s.reshape(rows // 8, 8, width), axis=0))
        top = jnp.max(top, axis=0, keepdims=True)
        total = jnp.zeros((8, width), f32)
        for block in range(blocks):
            span = slice(block * rows, (block + 1) * rows)
            p = jnp.exp2((s_ref[span, at] - top) * log_scale)
            total = total + jnp.sum(p.reshape(rows // 8, 8, width), axis=0)
            p_ref[span, at] = p.astype(bf16)
        inv = 1.0 / jnp.sum(total, axis=0, keepdims=True)
        inv_ref[:, at] = inv
        ot = jnp.dot(vt_ref[...], p_ref[:, at], preferred_element_type=f32) * inv
        ot = ot.astype(bf16)
        o_ref[group, at, :] = ot.T
        gt = g_ref[group, at, :].T
        gt_ref[:, at] = gt
        delta_ref[:, at] = jnp.sum(gt.astype(f32) * ot.astype(f32), axis=0, keepdims=True)
        gs_ref[:, at] = (gt.astype(f32) * inv).astype(bf16)
        qs_ref[:, at] = (qt.astype(f32) * inv).astype(bf16)

    def backward(group, first, width):
        at = slice(first, first + width)
        gt = gt_ref[:, at]
        delta = delta_ref[:, at]
        for block in range(blocks):
            span = slice(block * rows, (block + 1) * rows)
            dp = jnp.dot(kv_all[2 * group + 1, span, :], gt, preferred_element_type=f32)
            ds_ref[span, at] = (p_ref[span, at].astype(f32) * (dp - delta)).astype(bf16)
        dqt = jnp.dot(kt_ref[...], ds_ref[:, at], preferred_element_type=f32)
        dq_ref[group, at, :] = (dqt * (inv_ref[:, at] * scale)).astype(bf16).T

    def to_keys(unit, left, right):
        for block in range(blocks):
            span = slice(block * rows, (block + 1) * rows)
            part = lax.dot_general(
                left[span, :], right[...], (((1,), (1,)), ((), ())), preferred_element_type=f32
            )
            distance = blocks - 1 - block
            if distance % 2 == 0:
                part_own[unit, distance // 2] = part
            else:
                part_sib[unit, distance // 2] = part.astype(bf16)

    chunks = []
    for first in range(0, cols, 2 * rows):
        chunks.append((first, min(2 * rows, cols - first)))
    lag = BACK - 1

    def half(step, which, group):
        run = (group >= 0) & (group < groups) & COMPUTE
        unit = 2 * group + which
        last = len(chunks)
        kv_event(step, 0)

        @pl.when((group >= 0) & (group < groups))
        def _():
            @pl.when(unit == 0)
            def _():
                for slot in range(BACK):
                    doc_share(core + slot).wait_recv()
            if which == 0:
                for slot in range(BACK):
                    kv_share(unit, core + slot).wait_recv()
                for slot in range(BACK):
                    kv_share(unit + 1, core + slot).wait_recv()

        @pl.when(run)
        def _():
            if which == 0:
                pl.when(group == 0)(find_starts)
                kt_ref[...] = kv_all[2 * group].T
            else:
                pass

        for piece in range(last + 1):
            kv_event(step, piece + 1)
            sum_event(step, BACK - piece)

            @pl.when(run)
            def _():
                if which == 0:
                    if piece < last:
                        if piece == 0:
                            vt_ref[...] = kv_all[2 * group + 1].T
                        forward(group, *chunks[piece])
                    else:
                        to_keys(unit, p_ref, gs_ref)
                else:
                    if piece < last:
                        backward(group, *chunks[piece])
                    else:
                        to_keys(unit, ds_ref, qs_ref)
        sum_event(step, 0)

        @pl.when((group >= 0) & (group < groups))
        def _():
            part_share(unit).start()

    def body(turn, carry):
        half(2 * turn, 0, turn - lag)
        half(2 * turn + 1, 1, turn - lag)
        return carry

    turns = groups + lag + BACK - 1
    lax.fori_loop(0, turns, body, 0)

    def drain(ref, index):
        pltpu.make_async_copy(ref, ref, send_sems.at[index]).wait()

    moved = pl.ds(rows, BACK * rows)
    drain(kv_all.at[:, moved], 0)
    drain(kv_all.at[:, moved], 1)
    drain(doc_all.at[pl.ds(0, 8 * BACK)], 2)
    drain(doc_all.at[pl.ds(0, 8 * BACK)], 3)
    drain(part_sib, 4)
    drain(sums, 5)


def shards(queries, keys, values, grad_out, doc_ids):
    rows, heads, head = queries.shape
    groups = keys.shape[1]
    members = heads // groups
    units = 2 * groups
    cols = members * rows
    blocks = 2 * BACK + 1
    window = blocks * rows
    f32, bf16 = jnp.float32, jnp.bfloat16

    def by_group(array):
        return jnp.transpose(array, (1, 0, 2)).reshape(groups, cols, head)

    def by_row(array):
        return jnp.transpose(array.reshape(heads, rows, head), (1, 0, 2))

    pairs = jnp.stack([keys, values], axis=2)
    kv = jnp.transpose(pairs, (1, 2, 0, 3)).reshape(units, rows, head)
    docs = jnp.broadcast_to(doc_ids[None, :], (8, rows))
    vmem = pl.BlockSpec(memory_space=pltpu.VMEM)
    DMA = pltpu.SemaphoreType.DMA
    big = jax.ShapeDtypeStruct((groups, cols, head), bf16)
    out, dq, dkv = pl.pallas_call(
        kernel,
        out_shape=(big, big, jax.ShapeDtypeStruct((units, rows, head), bf16)),
        in_specs=[vmem] * 4,
        out_specs=[vmem] * 3,
        scratch_shapes=[
            pltpu.VMEM((units, window, head), bf16),
            pltpu.VMEM((8 * blocks, rows), jnp.int32),
            pltpu.VMEM((units, LINE, rows, head), f32),
            pltpu.VMEM((units, BACK, rows, head), bf16),
            pltpu.VMEM((units, LINE, rows, head), bf16),
            pltpu.VMEM((units, BACK, rows, head), bf16),
            pltpu.VMEM((units, BACK, rows, head), bf16),
            pltpu.VMEM((window, cols), f32),
            pltpu.VMEM((window, cols), bf16),
            pltpu.VMEM((window, cols), bf16),
            pltpu.VMEM((head, cols), bf16),
            pltpu.VMEM((head, cols), bf16),
            pltpu.VMEM((head, cols), bf16),
            pltpu.VMEM((head, cols), bf16),
            pltpu.VMEM((head, window), bf16),
            pltpu.VMEM((head, window), bf16),
            pltpu.VMEM((1, cols), jnp.int32),
            pltpu.VMEM((1, cols), f32),
            pltpu.VMEM((1, cols), f32),
            DMA((units, BACK)),
            DMA((units, BACK)),
            DMA((BACK,)),
            DMA((BACK,)),
            DMA((units,)),
            DMA((units, BACK)),
            DMA((6,)),
        ],
        compiler_params=pltpu.CompilerParams(
            collective_id=0, has_side_effects=True, vmem_limit_bytes=60 * 1024 * 1024
        ),
        name="ring_attention",
    )(by_group(queries), by_group(grad_out), kv, docs)
    dkv = jnp.transpose(dkv.reshape(groups, 2, rows, head), (1, 2, 0, 3))
    return (by_row(out), by_row(dq), dkv[1], dkv[0])


def solution(mesh):
    spec = P(("dp", "seq"), None, None)
    return jax.shard_map(
        shards,
        mesh=mesh,
        in_specs=(spec, spec, spec, spec, P(("dp", "seq"))),
        out_specs=(spec, spec, spec, spec),
        check_vma=False,
    )
```

time: 505 us -> 121 us (0.24); the launches traced: 496 us -> 121 us
  waiting for transfers between devices: 231 us -> 0 us
  Pallas kernels: 0 us -> 108 us
  local copies, waits for them, and re-layouts: 80 us -> 11.2 us
  matrix products: 62 us -> 0 us
  blocking collectives: 48 us -> 0 us
  starting transfers between devices: 44.8 us -> 0 us
  other arithmetic: 27.2 us -> 1.08 us
    all_to_all x8 -> x0, waiting for transfers between devices: 231 us -> none  [the longest x1 56.6 us: shards(): lax.all_to_all(dv_send, 'seq', split_axis=0, concat_axis=0, tiled=True)]
    pallas_call x0 -> x1, Pallas kernels: none -> 108 us  [shards(): pl.pallas_call(kernel, out_shape=(big, big, jax.ShapeDtypeStruct((units,...]
    dot_general x62 -> x0, matrix products: 62 us -> none  [the longest x10 11.2 us: attend(): jnp.dot(grad_score_low, k_block, preferred_element_type=jnp.float32)]
    all_gather x1 -> x0, blocking collectives: 48 us -> none  [shards(): doc_all = lax.all_gather(doc_ids, 'seq', axis=0, tiled=True)]
    all_to_all x8 -> x0, starting transfers between devices: 44.8 us -> none  [the longest x1 8.7 us: shards(): lax.all_to_all(q_send, 'seq', split_axis=0, concat_axis=0, tiled=True)]
    gather x10 -> x0, local copies, waits for them, and re-layouts: 39.5 us -> none  [the longest x4 20.5 us: kv_to_owners(): jnp.take(source, kv_table.reshape(-1), axis=1)]
    unnamed x206 -> x6, local copies, waits for them, and re-layouts: 20.5 us -> 0.09 us
    slice x34 -> x0, local copies, waits for them, and re-layouts: 16.8 us -> none  [the longest x2 4.02 us: attend(): q_block = query_rows[first_row:first_row + block_rows]]
  transfers between devices with their start and end apart: 8 -> 0, of which waited for: 7 -> 0; matrix products, arithmetic and copies ran while one was open for 19% -> 0% of each run, Pallas kernels for 0% -> 0%
where the time goes in v1:
time: 121 us
  Pallas kernels  108 us (89%)
  local copies, waits for them, and re-layouts  11.2 us (9%)
    pallas_call x1, Pallas kernels, shards(): pl.pallas_call(kernel, out_shape=(big, big, jax.ShapeDtypeStruct((units,...  108 us
    transpose x1, local copies, waits for them, and re-layouts, by_row(): return jnp.transpose(array.reshape(heads, rows, head), (1, 0, 2))  4.94 us
    transpose x2, local copies, waits for them, and re-layouts, by_group(): return jnp.transpose(array, (1, 0, 2)).reshape(groups, cols, head)  2.75 us

profile of v1, /device:TPU:12, one launch (start us, length us, event | category | flops | bytes accessed | tf_op | source)
XLA Modules:
  0.0 120.7 jit_solution(4850272358523487041)
XLA Ops:
  0.6 0.0 copy-start
  0.6 1.4 %broadcast_in_dim.2.doc_ref = s32[8,128]{1,0:T(8,128)} broadcast(s32[128]{0:T(128)} %param.9), dimensions={1} | broadcast | bytes 4608 | tf_op jit(solution)/shard_map/broadcast_in_dim | solution.py:313
  2.0 1.1 maximum_bitcast_fusion
  3.1 0.9 copy.11
  4.0 0.0 copy-done
  4.0 0.0 copy-start.1
  4.0 1.4 %copy.9 = bf16[40,128,128]{2,1,0:T(8,128)(2,1)} copy(bf16[40,128,128]{2,0,1:T(8,128)(2,1)S(1)} %bitcast.29) | data formatting | bytes 2621440 | tf_op jit(solution)/shard_map/transpose | solution.py:306
  5.4 0.1 copy-done.1
  5.4 1.4 %copy.10 = bf16[40,128,128]{2,1,0:T(8,128)(2,1)} copy(bf16[40,128,128]{2,0,1:T(8,128)(2,1)S(1)} %bitcast.30) | data formatting | bytes 2621440 | tf_op jit(solution)/shard_map/transpose | solution.py:306
  6.8 107.7 %ring_attention.1 = (bf16[8,640,128]{2,1,0:T(8,128)(2,1)}, bf16[8,640,128]{2,1,0:T(8,128)(2,1)}, bf16[16,128,128]{2,1,0:T(8,128)(2,1)}) custom-call(bf16[8,640,128]{2,1,0:T(8,128)(2,1)} %bitcast.23, bf16[8,640,128]{2,1,0:T(8,128)(2,1)} %bitcast.24, bf16[16,128,128]{2,1,0:T(8,128)(2,1)} %bitcast.26, s32[8,128]{1,0:T(8,128)} %broadcast_in_dim.2.doc_ref), custom_call_target="tpu_custom_call" | custom-call | tf_op jit(solution)/shard_map/ring_attention/pallas_call | solution.py:317
  114.5 0.0 copy-start.2
  114.5 4.9 %copy_bitcast_fusion = (bf16[128,40,128]{2,1,0:T(8,128)(2,1)}, bf16[128,40,128]{2,1,0:T(8,128)(2,1)}) fusion(bf16[40,128,128]{2,1,0:T(8,128)(2,1)} %bitcast.28, bf16[40,128,128]{2,1,0:T(8,128)(2,1)} %bitcast.27), kind=kLoop, calls=%fused_computation | loop fusion | bytes 5242880 | tf_op jit(solution)/shard_map/transpose | solution.py:309
  119.5 0.0 copy-done.2
  119.5 0.3 copy.18
  119.8 0.8 slice_bitcast_fusion
Async XLA Ops:
  0.6 3.4 %copy-start = (bf16[128,40,128]{2,1,0:T(8,128)(2,1)S(1)}, bf16[128,40,128]{2,1,0:T(8,128)(2,1)}, u32[]{:S(2)}) copy-start(bf16[128,40,128]{2,1,0:T(8,128)(2,1)} %param.5) | copy-start | bytes 3932164
  4.0 1.5 %copy-start.1 = (bf16[128,40,128]{2,1,0:T(8,128)(2,1)S(1)}, bf16[128,40,128]{2,1,0:T(8,128)(2,1)}, u32[]{:S(2)}) copy-start(bf16[128,40,128]{2,1,0:T(8,128)(2,1)} %param.8) | copy-start | bytes 3932164
  114.5 5.0 %copy-start.2 = (bf16[16,128,128]{2,1,0:T(8,128)(2,1)S(1)}, bf16[16,128,128]{2,1,0:T(8,128)(2,1)}, u32[]{:S(2)}) copy-start(bf16[16,128,128]{2,1,0:T(8,128)(2,1)} %get-tuple-element.9) | copy-start | bytes 1572868

commit v2 on v1

v2 whole, which is shorter than its diff:
```python
import functools
import math

import jax
import jax.numpy as jnp
from jax import lax
from jax.experimental import pallas as pl
from jax.experimental.pallas import tpu as pltpu
from jax.sharding import PartitionSpec as P

MESH = pl.DeviceIdType.MESH
BACK = 4
LINE = BACK + 1
PIECES = 4
SPANS = 3
KV_AT = (0, 4, 9, 14, 19)
SUM_AT = (22, 17, 12, 7, 2)
FIRST = 6
DOC_VALUES = 6


def rows_at(distance, rows):
    return pl.ds(pl.multiple_of((2 * BACK - distance) * rows, rows), rows)


def kernel(
    q_hbm, g_hbm, k_hbm, v_hbm, doc_hbm, o_hbm, dq_hbm, dk_hbm, dv_hbm,
    q16, g16, k16, v16, doc_row, q32, g32, k32, v32, qt_all, gt_all,
    kv_all, doc_all, part_own, part_sib, sib_got, sums, sums_got,
    s_ref, dp_ref, p_ref, ds_ref, qs_ref, gs_ref, kt_ref, vt_ref,
    start_ref, top_ref, delta_ref, inv_ref,
    kv_up_recv, kv_sib_recv, doc_up_recv, doc_sib_recv, sib_recv, sums_recv,
    send_sems, local_sems,
):
    units, window, head = kv_all.shape
    rows = doc_row.shape[1]
    groups = units // 2
    cols = s_ref.shape[1]
    members = cols // rows
    heads = members * groups
    blocks = window // rows
    size = lax.axis_size("seq")
    me = lax.axis_index("seq")
    core = lax.rem(me, 2)
    up = lax.rem(me + 2, size)
    down = lax.rem(me + size - 2, size)
    sib = me + 1 - 2 * core
    scale = 1.0 / math.sqrt(head)
    log_scale = scale * math.log2(math.e)
    f32, bf16 = jnp.float32, jnp.bfloat16

    barrier = pltpu.get_barrier_semaphore()
    for other in (up, down, sib):
        pl.semaphore_signal(barrier, inc=1, device_id={"seq": other}, device_id_type=MESH)

    loads = [
        pltpu.make_async_copy(src, dst, local_sems.at[index])
        for index, (src, dst) in enumerate(
            ((k_hbm, k16), (v_hbm, v16), (doc_hbm, doc_row), (q_hbm, q16), (g_hbm, g16))
        )
    ]
    for load in loads:
        load.start()
    sib_got[:, 0] = jnp.zeros((units, rows, head), bf16)
    sib_got[:, BACK] = jnp.zeros((units, rows, head), bf16)
    for load in loads[:3]:
        load.wait()
    k32[...] = k16[...].astype(f32)
    v32[...] = v16[...].astype(f32)
    own = slice(window - rows, window)
    for group in range(groups):
        kv_all[2 * group, own, :] = k32[pl.ds(group, rows, stride=groups), :].astype(bf16)
        kv_all[2 * group + 1, own, :] = v32[pl.ds(group, rows, stride=groups), :].astype(bf16)
    doc_all[16 * BACK : 16 * BACK + 8, :] = jnp.broadcast_to(doc_row[...], (8, rows))
    pl.semaphore_wait(barrier, 3)

    def remote(src, dst, send, recv, to):
        return pltpu.make_async_remote_copy(
            src_ref=src, dst_ref=dst, send_sem=send_sems.at[send], recv_sem=recv,
            device_id={"seq": to}, device_id_type=MESH,
        )

    def kv_up(unit, k):
        return remote(
            kv_all.at[unit, rows_at(2 * k, rows)], kv_all.at[unit, rows_at(2 * k + 2, rows)],
            0, kv_up_recv.at[unit, k], up,
        )

    def kv_share(unit, k):
        slot = k - core
        return remote(
            kv_all.at[unit, rows_at(2 * k, rows)], kv_all.at[unit, rows_at(2 * slot + 1, rows)],
            1, kv_sib_recv.at[unit, slot], sib,
        )

    def doc_up(k):
        return remote(
            doc_all.at[rows_at(2 * k, 8)], doc_all.at[rows_at(2 * k + 2, 8)],
            2, doc_up_recv.at[k], up,
        )

    def doc_share(k):
        slot = k - core
        return remote(
            doc_all.at[rows_at(2 * k, 8)], doc_all.at[rows_at(2 * slot + 1, 8)],
            3, doc_sib_recv.at[slot], sib,
        )

    def part_share(unit):
        return remote(
            part_sib.at[unit], sib_got.at[unit, pl.ds(1 - core, BACK)],
            4, sib_recv.at[unit], sib,
        )

    def sum_down(unit, j):
        return remote(
            sums.at[unit, j - 1], sums_got.at[unit, j - 1],
            5, sums_recv.at[unit, j - 1], down,
        )

    def kv_event(step, k):
        unit = step - KV_AT[k] // PIECES

        @pl.when((unit >= 0) & (unit < units))
        def _():
            if k > 0:
                @pl.when(unit == 0)
                def _():
                    doc_up(k - 1).wait_recv()
                kv_up(unit, k - 1).wait_recv()
            if k < BACK:
                @pl.when(unit == 0)
                def _():
                    doc_up(k).start()
                kv_up(unit, k).start()

            def share():
                @pl.when(unit == 0)
                def _():
                    doc_share(k).start()
                kv_share(unit, k).start()

            if k == 0:
                pl.when(core == 0)(share)
            elif k == BACK:
                pl.when(core == 1)(share)
            else:
                share()

    def sum_event(step, which, j):
        back = FIRST + 1 + SUM_AT[j] // PIECES
        unit = step - back

        @pl.when((unit >= 0) & (unit < units))
        def _():
            if j == BACK:
                part_share(unit).wait_recv()
            total = part_own[unit, j] + sib_got[unit, j].astype(f32)
            if j < BACK:
                sum_down(unit, j + 1).wait_recv()
                total = total + sums_got[unit, j].astype(f32)
            if j > 0:
                sums[unit, j - 1] = total.astype(bf16)
                sum_down(unit, j).start()
            elif (which - back) % 2 == 1:
                k32[pl.ds(unit // 2, rows, stride=groups), :] = total * scale
            else:
                v32[pl.ds(unit // 2, rows, stride=groups), :] = total

    def find_starts():
        docs = doc_row[...]
        old = lax.broadcasted_iota(jnp.int32, (8 * blocks, rows), 0) // 8
        old = old + (me - 2 * BACK) < 0
        all_docs = jnp.where(old, -1, doc_all[...])
        start = jnp.zeros((1, rows), jnp.int32)
        for value in range(DOC_VALUES):
            less = jnp.where(all_docs < value, 1, 0)
            count = jnp.sum(jnp.sum(less, axis=0, keepdims=True), axis=1, keepdims=True) // 8
            start = jnp.where(docs == value, count, start)
        for member in range(members):
            start_ref[:, member * rows : (member + 1) * rows] = start

    def widen(source, dest):
        def move(index, carry):
            at = pl.ds(pl.multiple_of(index * 256, 256), 256)
            dest[at, :] = source[at, :].astype(dest.dtype)
            return carry

        lax.fori_loop(0, source.shape[0] // 256, move, 0)

    def by_row(source, dest):
        def move(index, carry):
            pair = [
                source[pl.ds(2 * index + odd, heads, stride=rows), :] for odd in (0, 1)
            ]
            at = pl.ds(pl.multiple_of(2 * heads * index, 2 * heads), 2 * heads)
            dest[at, :] = jnp.concatenate(pair, axis=0).astype(dest.dtype)
            return carry

        lax.fori_loop(0, rows // 2, move, 0)

    def prepare(number):
        for index in (2 * number, 2 * number + 1):
            every = pl.ds(index, rows, stride=heads)
            qt_all[index] = q32[every, :].T.astype(bf16)
            gt_all[index] = g32[every, :].T.astype(bf16)

    def pick(ref, group):
        return jnp.concatenate([ref[group * members + index] for index in range(members)], axis=1)

    def put(ref, group, value):
        for index in range(members):
            at = pl.ds(pl.multiple_of((group * members + index) * rows, rows), rows)
            ref[at, :] = value[:, index * rows : (index + 1) * rows].T

    def score(group):
        start = start_ref[...]
        s_ref[...] = jnp.dot(kv_all[2 * group], pick(qt_all, group), preferred_element_type=f32)
        top = jnp.full((8, cols), -jnp.inf, f32)
        for block in range(blocks):
            span = slice(block * rows, (block + 1) * rows)
            where = block * rows + lax.broadcasted_iota(jnp.int32, (rows, cols), 0)
            allowed = where >= start
            if block == blocks - 1:
                mine = lax.broadcasted_iota(jnp.int32, (rows, cols), 1) % rows
                allowed = allowed & (where - block * rows <= mine)
            s = jnp.where(allowed, s_ref[span], -jnp.inf)
            s_ref[span] = s
            top = jnp.maximum(top, jnp.max(s.reshape(rows // 8, 8, cols), axis=0))
        top_ref[...] = jnp.max(top, axis=0, keepdims=True)

    def raise_scores(group):
        top = top_ref[...]
        gt = pick(gt_all, group)
        total = jnp.zeros((8, cols), f32)
        for first in range(0, blocks, SPANS):
            wide = slice(first * rows, (first + SPANS) * rows)
            dp_ref[wide] = jnp.dot(
                kv_all[2 * group + 1, wide], gt, preferred_element_type=f32
            )
            for block in range(first, first + SPANS):
                span = slice(block * rows, (block + 1) * rows)
                p = jnp.exp2((s_ref[span] - top) * log_scale)
                total = total + jnp.sum(p.reshape(rows // 8, 8, cols), axis=0)
                p_ref[span] = p.astype(bf16)
        inv_ref[...] = 1.0 / jnp.sum(total, axis=0, keepdims=True)

    def attend(group):
        inv = inv_ref[...]
        ot = jnp.dot(vt_ref[...], p_ref[...], preferred_element_type=f32) * inv
        ot = ot.astype(bf16).astype(f32)
        put(q32, group, ot)
        gt = pick(gt_all, group).astype(f32)
        delta_ref[...] = jnp.sum(gt * ot, axis=0, keepdims=True)
        gs_ref[...] = (gt * inv).astype(bf16)
        qs_ref[...] = (pick(qt_all, group).astype(f32) * inv).astype(bf16)

    def grad_scores():
        delta = delta_ref[...]
        for block in range(blocks):
            span = slice(block * rows, (block + 1) * rows)
            ds_ref[span] = (p_ref[span].astype(f32) * (dp_ref[span] - delta)).astype(bf16)

    def to_queries(group):
        dqt = jnp.dot(kt_ref[...], ds_ref[...], preferred_element_type=f32)
        put(g32, group, dqt * (inv_ref[...] * scale))

    def to_keys(unit, left, right):
        part = lax.dot_general(
            left[...], right[...], (((1,), (1,)), ((), ())), preferred_element_type=f32
        )
        for block in range(blocks):
            span = slice(block * rows, (block + 1) * rows)
            distance = blocks - 1 - block
            if distance % 2 == 0:
                part_own[unit, distance // 2] = part[span]
            else:
                part_sib[unit, distance // 2] = part[span].astype(bf16)

    lag = FIRST // 2
    prep_steps = heads // (2 * PIECES)

    def half(step, which, group):
        run = (group >= 0) & (group < groups)
        unit = 2 * group + which
        kv_event(step, 0)
        if which == 0:
            @pl.when(step == 0)
            def _():
                loads[3].wait()
                loads[4].wait()
                widen(q16, q32)
                widen(g16, g32)

            @pl.when(run)
            def _():
                @pl.when(unit == 0)
                def _():
                    for slot in range(BACK):
                        doc_share(core + slot).wait_recv()
                    find_starts()

                for slot in range(BACK):
                    kv_share(unit, core + slot).wait_recv()
                kt_ref[...] = kv_all[unit].T

        for piece in range(PIECES):
            for k in range(1, LINE):
                if KV_AT[k] % PIECES == piece:
                    kv_event(step, k)
            for j in range(BACK, -1, -1):
                if SUM_AT[j] % PIECES == piece:
                    sum_event(step, which, j)

            @pl.when(step < prep_steps)
            def _():
                prepare(step * PIECES + piece)

            @pl.when(run)
            def _():
                if which == 0:
                    if piece == 0:
                        score(group)
                    elif piece == 1:
                        for slot in range(BACK):
                            kv_share(unit + 1, core + slot).wait_recv()
                        raise_scores(group)
                    elif piece == 2:
                        vt_ref[...] = kv_all[unit + 1].T
                        attend(group)
                    else:
                        to_keys(unit, p_ref, gs_ref)
                else:
                    if piece == 0:
                        grad_scores()
                    elif piece == 1:
                        to_queries(group)
                    elif piece == 2:
                        to_keys(unit, ds_ref, qs_ref)

        @pl.when(run)
        def _():
            part_share(unit).start()

        @pl.when(group == groups)
        def _():
            if which == 0:
                by_row(q32, q16)
                pltpu.make_async_copy(q16, o_hbm, local_sems.at[0]).start()
            else:
                by_row(g32, g16)
                pltpu.make_async_copy(g16, dq_hbm, local_sems.at[1]).start()

    def body(turn, carry):
        half(2 * turn, 0, turn - lag)
        half(2 * turn + 1, 1, turn - lag)
        return carry

    steps = units + FIRST + 1 + max(SUM_AT) // PIECES
    lax.fori_loop(0, -(-steps // 2), body, 0)

    k16[...] = k32[...].astype(bf16)
    v16[...] = v32[...].astype(bf16)
    stores = [
        pltpu.make_async_copy(q16, o_hbm, local_sems.at[0]),
        pltpu.make_async_copy(g16, dq_hbm, local_sems.at[1]),
        pltpu.make_async_copy(k16, dk_hbm, local_sems.at[2]),
        pltpu.make_async_copy(v16, dv_hbm, local_sems.at[3]),
    ]
    stores[2].start()
    stores[3].start()

    def drain(ref, index):
        pltpu.make_async_copy(ref, ref, send_sems.at[index]).wait()

    moved = pl.ds(rows, BACK * rows)
    drain(kv_all.at[:, moved], 0)
    drain(kv_all.at[:, moved], 1)
    drain(doc_all.at[pl.ds(0, 8 * BACK)], 2)
    drain(doc_all.at[pl.ds(0, 8 * BACK)], 3)
    drain(part_sib, 4)
    drain(sums, 5)
    for store in stores:
        store.wait()


def settle(*refs):
    count = len(refs) // 2
    for index in range(count):
        refs[count + index][...] = refs[index][...]


def shards(queries, keys, values, grad_out, doc_ids):
    rows, heads, head = queries.shape
    groups = keys.shape[1]
    members = heads // groups
    units = 2 * groups
    cols = members * rows
    blocks = 2 * BACK + 1
    window = blocks * rows
    f32, bf16 = jnp.float32, jnp.bfloat16

    def flat(array):
        return array.reshape(-1, head)

    def by_part(shape):
        return pl.BlockSpec((shape[0] // 4, head), lambda index: (index, 0))

    anywhere = pl.BlockSpec(memory_space=pl.ANY)
    DMA = pltpu.SemaphoreType.DMA
    big, small = (heads * rows, head), (groups * rows, head)
    shapes = [jax.ShapeDtypeStruct(shape, bf16) for shape in (big, big, small, small)]
    results = pl.pallas_call(
        kernel,
        out_shape=shapes,
        in_specs=[anywhere] * 5,
        out_specs=[anywhere] * 4,
        scratch_shapes=[
            pltpu.VMEM(big, bf16),
            pltpu.VMEM(big, bf16),
            pltpu.VMEM(small, bf16),
            pltpu.VMEM(small, bf16),
            pltpu.VMEM((1, rows), jnp.int32),
            pltpu.VMEM(big, f32),
            pltpu.VMEM(big, f32),
            pltpu.VMEM(small, f32),
            pltpu.VMEM(small, f32),
            pltpu.VMEM((heads, head, rows), bf16),
            pltpu.VMEM((heads, head, rows), bf16),
            pltpu.VMEM((units, window, head), bf16),
            pltpu.VMEM((8 * blocks, rows), jnp.int32),
            pltpu.VMEM((units, LINE, rows, head), f32),
            pltpu.VMEM((units, BACK, rows, head), bf16),
            pltpu.VMEM((units, LINE, rows, head), bf16),
            pltpu.VMEM((units, BACK, rows, head), bf16),
            pltpu.VMEM((units, BACK, rows, head), bf16),
            pltpu.VMEM((window, cols), f32),
            pltpu.VMEM((window, cols), f32),
            pltpu.VMEM((window, cols), bf16),
            pltpu.VMEM((window, cols), bf16),
            pltpu.VMEM((head, cols), bf16),
            pltpu.VMEM((head, cols), bf16),
            pltpu.VMEM((head, window), bf16),
            pltpu.VMEM((head, window), bf16),
            pltpu.VMEM((1, cols), jnp.int32),
            pltpu.VMEM((1, cols), f32),
            pltpu.VMEM((1, cols), f32),
            pltpu.VMEM((1, cols), f32),
            DMA((units, BACK)),
            DMA((units, BACK)),
            DMA((BACK,)),
            DMA((BACK,)),
            DMA((units,)),
            DMA((units, BACK)),
            DMA((6,)),
            DMA((5,)),
        ],
        compiler_params=pltpu.CompilerParams(
            collective_id=0, has_side_effects=True, vmem_limit_bytes=60 * 1024 * 1024
        ),
        name="ring_attention",
    )(flat(queries), flat(grad_out), flat(keys), flat(values), doc_ids.reshape(1, rows))
    out, dq, dk, dv = pl.pallas_call(
        settle,
        out_shape=shapes,
        grid=(4,),
        in_specs=[by_part(shape) for shape in (big, big, small, small)],
        out_specs=[by_part(shape) for shape in (big, big, small, small)],
        name="settle",
    )(*results)
    return (
        out.reshape(rows, heads, head), dq.reshape(rows, heads, head),
        dk.reshape(rows, groups, head), dv.reshape(rows, groups, head),
    )


def solution(mesh):
    spec = P(("dp", "seq"), None, None)
    return jax.shard_map(
        shards,
        mesh=mesh,
        in_specs=(spec, spec, spec, spec, P(("dp", "seq"))),
        out_specs=(spec, spec, spec, spec),
        check_vma=False,
    )
```

time: 121 us -> 91.8 us (0.76)
  Pallas kernels: 108 us -> 91 us
  local copies, waits for them, and re-layouts: 11.2 us -> 0 us
    pallas_call x1 -> x2, Pallas kernels: 108 us -> 91 us  [the longest x1 87 us: shards(): pl.pallas_call(kernel, out_shape=shapes, in_specs=[anywhere] * 5, out_spe...]
    transpose x4 -> x0, local copies, waits for them, and re-layouts: 8.61 us -> none  [the longest x1 4.94 us: by_row(): return jnp.transpose(array.reshape(heads, rows, head), (1, 0, 2))]
    broadcast_in_dim x1 -> x0, local copies, waits for them, and re-layouts: 1.35 us -> none  [shards(): docs = jnp.broadcast_to(doc_ids[None, :], (8, rows))]
where the time goes in v2:
time: 91.8 us; the launch traced here: 91.7 us
  Pallas kernels  91 us (99%)
    pallas_call x1, Pallas kernels, shards(): pl.pallas_call(kernel, out_shape=shapes, in_specs=[anywhere] * 5, out_spe...  87 us
    pallas_call x1, Pallas kernels, shards(): pl.pallas_call(settle, out_shape=shapes, grid=(4,), in_specs=[by_part(sha...  4.06 us

profile of v2, /device:TPU:12, one launch (start us, length us, event | category | flops | bytes accessed | tf_op | source)
XLA Modules:
  0.0 91.7 jit_solution(17725365787375677490)
XLA Ops:
  0.6 87.0 %ring_attention.1 = (bf16[5120,128]{1,0:T(8,128)(2,1)}, bf16[5120,128]{1,0:T(8,128)(2,1)}, bf16[1024,128]{1,0:T(8,128)(2,1)}, bf16[1024,128]{1,0:T(8,128)(2,1)}) custom-call(bf16[5120,128]{1,0:T(8,128)(2,1)} %bitcast.9, bf16[5120,128]{1,0:T(8,128)(2,1)} %bitcast.10, bf16[1024,128]{1,0:T(8,128)(2,1)} %bitcast.11, bf16[1024,128]{1,0:T(8,128)(2,1)} %bitcast.12, ...), custom_call_target="tpu_custom_call" | custom-call | tf_op jit(solution)/shard_map/ring_attention/pallas_call | solution.py:413
  87.6 4.1 %settle.1 = (bf16[5120,128]{1,0:T(8,128)(2,1)}, bf16[5120,128]{1,0:T(8,128)(2,1)}, bf16[1024,128]{1,0:T(8,128)(2,1)}, bf16[1024,128]{1,0:T(8,128)(2,1)}) custom-call(bf16[5120,128]{1,0:T(8,128)(2,1)} %get-tuple-element.12.refs_0_, bf16[5120,128]{1,0:T(8,128)(2,1)} %get-tuple-element.13.refs_1_, bf16[1024,128]{1,0:T(8,128)(2,1)} %get-tuple-element.14.refs_2_, ...), custom_call_target="tpu_custom_call" | custom-call | tf_op jit(solution)/shard_map/settle/pallas_call | solution.py:463

commit v3 on v2

--- a/solution.py
+++ b/solution.py
@@ -13,9 +13,11 @@
 LINE = BACK + 1
 PIECES = 4
 SPANS = 3
-KV_AT = (0, 4, 9, 14, 19)
+FIRST = 6
+KV_AT = (-5, 1, 7, 13, 19)
 SUM_AT = (22, 17, 12, 7, 2)
-FIRST = 6
+SUM_LATE = (12, 3, 7, 2, 2)
+LATE = 2
 DOC_VALUES = 6
 
 
@@ -44,13 +46,15 @@
     core = lax.rem(me, 2)
     up = lax.rem(me + 2, size)
     down = lax.rem(me + size - 2, size)
+    up2 = lax.rem(me + 4, size)
+    down2 = lax.rem(me + size - 4, size)
     sib = me + 1 - 2 * core
     scale = 1.0 / math.sqrt(head)
     log_scale = scale * math.log2(math.e)
     f32, bf16 = jnp.float32, jnp.bfloat16
 
     barrier = pltpu.get_barrier_semaphore()
-    for other in (up, down, sib):
+    for other in (up, down, up2, down2, sib):
         pl.semaphore_signal(barrier, inc=1, device_id={"seq": other}, device_id_type=MESH)
 
     loads = [
@@ -72,7 +76,7 @@
         kv_all[2 * group, own, :] = k32[pl.ds(group, rows, stride=groups), :].astype(bf16)
         kv_all[2 * group + 1, own, :] = v32[pl.ds(group, rows, stride=groups), :].astype(bf16)
     doc_all[16 * BACK : 16 * BACK + 8, :] = jnp.broadcast_to(doc_row[...], (8, rows))
-    pl.semaphore_wait(barrier, 3)
+    pl.semaphore_wait(barrier, 5)
 
     def remote(src, dst, send, recv, to):
         return pltpu.make_async_remote_copy(
@@ -112,60 +116,53 @@
             4, sib_recv.at[unit], sib,
         )
 
-    def sum_down(unit, j):
+    def sum_down(unit, j, hops):
         return remote(
             sums.at[unit, j - 1], sums_got.at[unit, j - 1],
-            5, sums_recv.at[unit, j - 1], down,
-        )
-
-    def kv_event(step, k):
-        unit = step - KV_AT[k] // PIECES
-
-        @pl.when((unit >= 0) & (unit < units))
-        def _():
-            if k > 0:
-                @pl.when(unit == 0)
-                def _():
-                    doc_up(k - 1).wait_recv()
-                kv_up(unit, k - 1).wait_recv()
-            if k < BACK:
-                @pl.when(unit == 0)
-                def _():
-                    doc_up(k).start()
-                kv_up(unit, k).start()
-
-            def share():
-                @pl.when(unit == 0)
-                def _():
-                    doc_share(k).start()
-                kv_share(unit, k).start()
-
-            if k == 0:
-                pl.when(core == 0)(share)
-            elif k == BACK:
-                pl.when(core == 1)(share)
-            else:
-                share()
-
-    def sum_event(step, which, j):
-        back = FIRST + 1 + SUM_AT[j] // PIECES
-        unit = step - back
-
-        @pl.when((unit >= 0) & (unit < units))
-        def _():
-            if j == BACK:
-                part_share(unit).wait_recv()
-            total = part_own[unit, j] + sib_got[unit, j].astype(f32)
-            if j < BACK:
-                sum_down(unit, j + 1).wait_recv()
-                total = total + sums_got[unit, j].astype(f32)
-            if j > 0:
-                sums[unit, j - 1] = total.astype(bf16)
-                sum_down(unit, j).start()
-            elif (which - back) % 2 == 1:
-                k32[pl.ds(unit // 2, rows, stride=groups), :] = total * scale
-            else:
-                v32[pl.ds(unit // 2, rows, stride=groups), :] = total
+            5, sums_recv.at[unit, j - 1], down if hops == 1 else down2,
+        )
+
+    def kv_event(unit, k):
+        with_docs = isinstance(unit, int) and unit == 0
+        if k > 0:
+            if with_docs:
+                doc_up(k - 1).wait_recv()
+            kv_up(unit, k - 1).wait_recv()
+        if k < BACK:
+            if with_docs:
+                doc_up(k).start()
+            kv_up(unit, k).start()
+
+        def share():
+            if with_docs:
+                doc_share(k).start()
+            kv_share(unit, k).start()
+
+        if k == 0:
+            pl.when(core == 0)(share)
+        elif k == BACK:
+            pl.when(core == 1)(share)
+        else:
+            share()
+
+    def sum_event(unit, kind, j, late):
+        if j == BACK:
+            part_share(unit).wait_recv()
+        total = part_own[unit, j] + sib_got[unit, j].astype(f32)
+        if late:
+            sources, hops = {2: (2, 3), 0: (0, 1)}.get(j, ()), 2 - j % 2
+        else:
+            sources, hops = (j,) if j < BACK else (), 1
+        for source in sources:
+            sum_down(unit, source + 1, 1).wait_recv()
+            total = total + sums_got[unit, source].astype(f32)
+        if j > 0:
+            sums[unit, j - 1] = total.astype(bf16)
+            sum_down(unit, j, hops).start()
+        elif kind == 1:
+            k32[pl.ds(unit // 2, rows, stride=groups), :] = total * scale
+        else:
+            v32[pl.ds(unit // 2, rows, stride=groups), :] = total
 
     def find_starts():
         docs = doc_row[...]
@@ -200,7 +197,7 @@
         lax.fori_loop(0, rows // 2, move, 0)
 
     def prepare(number):
-        for index in (2 * number, 2 * number + 1):
+        for index in range(min(3 * number, heads), min(3 * number + 3, heads)):
             every = pl.ds(index, rows, stride=heads)
             qt_all[index] = q32[every, :].T.astype(bf16)
             gt_all[index] = g32[every, :].T.astype(bf16)
@@ -277,49 +274,58 @@
             else:
                 part_sib[unit, distance // 2] = part[span].astype(bf16)
 
-    lag = FIRST // 2
-    prep_steps = heads // (2 * PIECES)
+    begin, end = PIECES * FIRST, PIECES * (FIRST + units)
+    before = {}
+    for unit in range(units):
+        for k in range(LINE):
+            when = PIECES * unit + KV_AT[k]
+            if when < begin:
+                before.setdefault(max(when, 0), []).append((unit, k))
+    for now in range(begin):
+        for unit, k in before.get(now, ()):
+            kv_event(unit, k)
+        if now == 0:
+            loads[3].wait()
+            loads[4].wait()
+            widen(q16, q32)
+            widen(g16, g32)
+        prepare(now)
+    for slot in range(BACK):
+        doc_share(core + slot).wait_recv()
+    find_starts()
 
     def half(step, which, group):
-        run = (group >= 0) & (group < groups)
-        unit = 2 * group + which
-        kv_event(step, 0)
-        if which == 0:
-            @pl.when(step == 0)
-            def _():
-                loads[3].wait()
-                loads[4].wait()
-                widen(q16, q32)
-                widen(g16, g32)
-
-            @pl.when(run)
-            def _():
-                @pl.when(unit == 0)
-                def _():
-                    for slot in range(BACK):
-                        doc_share(core + slot).wait_recv()
-                    find_starts()
-
-                for slot in range(BACK):
-                    kv_share(unit, core + slot).wait_recv()
-                kt_ref[...] = kv_all[unit].T
-
         for piece in range(PIECES):
-            for k in range(1, LINE):
+            for k in range(LINE):
+                unit = step - KV_AT[k] // PIECES
                 if KV_AT[k] % PIECES == piece:
-                    kv_event(step, k)
+                    @pl.when(unit < units)
+                    def _():
+                        kv_event(unit, k)
+
             for j in range(BACK, -1, -1):
-                if SUM_AT[j] % PIECES == piece:
-                    sum_event(step, which, j)
-
-            @pl.when(step < prep_steps)
-            def _():
-                prepare(step * PIECES + piece)
-
-            @pl.when(run)
+                for late, table in enumerate((SUM_AT, SUM_LATE)):
+                    back = FIRST + 1 + table[j] // PIECES
+                    if table[j] % PIECES != piece or table[j] > PIECES and late:
+                        continue
+                    unit = step - back
+                    if late:
+                        live = (unit >= units - LATE) & (unit < units)
+                    else:
+                        live = (unit >= 0) & (unit < units - LATE)
+
+                    @pl.when(live)
+                    def _():
+                        sum_event(unit, (which - back) % 2, j, late == 1)
+
+            unit = 2 * group + which
+
+            @pl.when(me >= 0)
             def _():
                 if which == 0:
                     if piece == 0:
+                        for slot in range(BACK):
+                            kv_share(unit, core + slot).wait_recv()
                         score(group)
                     elif piece == 1:
                         for slot in range(BACK):
@@ -333,31 +339,36 @@
                 else:
                     if piece == 0:
                         grad_scores()
+                        kt_ref[...] = kv_all[unit - 1].T
                     elif piece == 1:
                         to_queries(group)
                     elif piece == 2:
                         to_keys(unit, ds_ref, qs_ref)
-
-        @pl.when(run)
-        def _():
-            part_share(unit).start()
-
-        @pl.when(group == groups)
-        def _():
-            if which == 0:
-                by_row(q32, q16)
-                pltpu.make_async_copy(q16, o_hbm, local_sems.at[0]).start()
-            else:
-                by_row(g32, g16)
-                pltpu.make_async_copy(g16, dq_hbm, local_sems.at[1]).start()
-
-    def body(turn, carry):
-        half(2 * turn, 0, turn - lag)
-        half(2 * turn + 1, 1, turn - lag)
+        part_share(unit).start()
+
+    def body(group, carry):
+        half(2 * group + FIRST, 0, group)
+        half(2 * group + FIRST + 1, 1, group)
         return carry
 
-    steps = units + FIRST + 1 + max(SUM_AT) // PIECES
-    lax.fori_loop(0, -(-steps // 2), body, 0)
+    lax.fori_loop(0, groups, body, 0)
+
+    after = {}
+    for unit in range(units):
+        late = unit >= units - LATE
+        table = SUM_LATE if late else SUM_AT
+        for j in range(BACK, -1, -1):
+            when = PIECES * (FIRST + 1 + unit) + table[j]
+            if when >= end or late and table[j] > PIECES:
+                after.setdefault(when, []).append((unit, j))
+    moves = [(q32, q16, o_hbm, 0), (g32, g16, dq_hbm, 1)]
+    for now in sorted(after):
+        for unit, j in after[now]:
+            sum_event(unit, unit % 2, j, unit >= units - LATE)
+        if moves and now >= end + 2:
+            wide, narrow, result, index = moves.pop(0)
+            by_row(wide, narrow)
+            pltpu.make_async_copy(narrow, result, local_sems.at[index]).start()
 
     k16[...] = k32[...].astype(bf16)
     v16[...] = v32[...].astype(bf16)
@@ -385,9 +396,29 @@
 
 
 def settle(*refs):
-    count = len(refs) // 2
+    count = 4
+    sources, results, held = refs[:count], refs[count : 2 * count], refs[2 * count : 3 * count]
+    sems = refs[-1]
+    pairs = []
     for index in range(count):
-        refs[count + index][...] = refs[index][...]
+        size = held[index].shape[0]
+        part = min(size, 1280)
+        for first in range(0, size, part):
+            at = pl.ds(first, part)
+            inward = pltpu.make_async_copy(
+                sources[index].at[at], held[index].at[at], sems.at[0, len(pairs)]
+            )
+            outward = pltpu.make_async_copy(
+                held[index].at[at], results[index].at[at], sems.at[1, len(pairs)]
+            )
+            pairs.append((inward, outward))
+    for inward, outward in pairs:
+        inward.start()
+    for inward, outward in pairs:
+        inward.wait()
+        outward.start()
+    for inward, outward in pairs:
+        outward.wait()
 
 
 def shards(queries, keys, values, grad_out, doc_ids):
@@ -402,9 +433,6 @@
 
     def flat(array):
         return array.reshape(-1, head)
-
-    def by_part(shape):
-        return pl.BlockSpec((shape[0] // 4, head), lambda index: (index, 0))
 
     anywhere = pl.BlockSpec(memory_space=pl.ANY)
     DMA = pltpu.SemaphoreType.DMA
@@ -463,9 +491,10 @@
     out, dq, dk, dv = pl.pallas_call(
         settle,
         out_shape=shapes,
-        grid=(4,),
-        in_specs=[by_part(shape) for shape in (big, big, small, small)],
-        out_specs=[by_part(shape) for shape in (big, big, small, small)],
+        in_specs=[anywhere] * 4,
+        out_specs=[anywhere] * 4,
+        scratch_shapes=[pltpu.VMEM(shape, bf16) for shape in (big, big, small, small)]
+        + [DMA((2, 10))],
         name="settle",
     )(*results)
     return (

time: 91.8 us -> 90.1 us (0.981)
  Pallas kernels: 91 us -> 89.3 us
    pallas_call x1, Pallas kernels: 4.06 us -> 2.8 us  [shards(): pl.pallas_call(settle, out_shape=shapes, in_specs=[anywhere] * 4, out_spe...]
where the time goes in v3:
time: 90.1 us; the launch traced here: 89.9 us
  Pallas kernels  89.3 us (99%)
    pallas_call x1, Pallas kernels, shards(): pl.pallas_call(kernel, out_shape=shapes, in_specs=[anywhere] * 5, out_spe...  86.5 us
    pallas_call x1, Pallas kernels, shards(): pl.pallas_call(settle, out_shape=shapes, in_specs=[anywhere] * 4, out_spe...  2.8 us

profile of v3, /device:TPU:12, one launch (start us, length us, event | category | flops | bytes accessed | tf_op | source)
XLA Modules:
  0.0 89.9 jit_solution(7737026242038011537)
XLA Ops:
  0.6 86.5 %ring_attention.1 = (bf16[5120,128]{1,0:T(8,128)(2,1)}, bf16[5120,128]{1,0:T(8,128)(2,1)}, bf16[1024,128]{1,0:T(8,128)(2,1)}, bf16[1024,128]{1,0:T(8,128)(2,1)}) custom-call(bf16[5120,128]{1,0:T(8,128)(2,1)} %bitcast.9, bf16[5120,128]{1,0:T(8,128)(2,1)} %bitcast.10, bf16[1024,128]{1,0:T(8,128)(2,1)} %bitcast.11, bf16[1024,128]{1,0:T(8,128)(2,1)} %bitcast.12, ...), custom_call_target="tpu_custom_call" | custom-call | tf_op jit(solution)/shard_map/ring_attention/pallas_call | solution.py:441
  87.1 2.8 %settle.1 = (bf16[5120,128]{1,0:T(8,128)(2,1)}, bf16[5120,128]{1,0:T(8,128)(2,1)}, bf16[1024,128]{1,0:T(8,128)(2,1)}, bf16[1024,128]{1,0:T(8,128)(2,1)}) custom-call(bf16[5120,128]{1,0:T(8,128)(2,1)} %get-tuple-element.12.refs_0_, bf16[5120,128]{1,0:T(8,128)(2,1)} %get-tuple-element.13.refs_1_, bf16[1024,128]{1,0:T(8,128)(2,1)} %get-tuple-element.14.refs_2_, ...), custom_call_target="tpu_custom_call" | custom-call | tf_op jit(solution)/shard_map/settle/pallas_call | solution.py:491

commit v4 on v3

--- a/solution.py
+++ b/solution.py
@@ -362,16 +362,19 @@
             if when >= end or late and table[j] > PIECES:
                 after.setdefault(when, []).append((unit, j))
     moves = [(q32, q16, o_hbm, 0), (g32, g16, dq_hbm, 1)]
+    values_end = max(now for now in after if any(unit % 2 == 0 for unit, j in after[now]))
     for now in sorted(after):
         for unit, j in after[now]:
             sum_event(unit, unit % 2, j, unit >= units - LATE)
+        if now == values_end:
+            v16[...] = v32[...].astype(bf16)
+            pltpu.make_async_copy(v16, dv_hbm, local_sems.at[3]).start()
         if moves and now >= end + 2:
             wide, narrow, result, index = moves.pop(0)
             by_row(wide, narrow)
             pltpu.make_async_copy(narrow, result, local_sems.at[index]).start()
 
     k16[...] = k32[...].astype(bf16)
-    v16[...] = v32[...].astype(bf16)
     stores = [
         pltpu.make_async_copy(q16, o_hbm, local_sems.at[0]),
         pltpu.make_async_copy(g16, dq_hbm, local_sems.at[1]),
@@ -379,7 +382,6 @@
         pltpu.make_async_copy(v16, dv_hbm, local_sems.at[3]),
     ]
     stores[2].start()
-    stores[3].start()
 
     def drain(ref, index):
         pltpu.make_async_copy(ref, ref, send_sems.at[index]).wait()
@@ -402,7 +404,7 @@
     pairs = []
     for index in range(count):
         size = held[index].shape[0]
-        part = min(size, 1280)
+        part = min(size, 512)
         for first in range(0, size, part):
             at = pl.ds(first, part)
             inward = pltpu.make_async_copy(
@@ -494,7 +496,7 @@
         in_specs=[anywhere] * 4,
         out_specs=[anywhere] * 4,
         scratch_shapes=[pltpu.VMEM(shape, bf16) for shape in (big, big, small, small)]
-        + [DMA((2, 10))],
+        + [DMA((2, 24))],
         name="settle",
     )(*results)
     return (

time: 90.1 us -> 90.4 us (level)
  no operation moved by 1% of the time
where the time goes in v4:
time: 90.4 us; the launch traced here: 90.3 us
  Pallas kernels  89.7 us (99%)
    pallas_call x1, Pallas kernels, shards(): pl.pallas_call(kernel, out_shape=shapes, in_specs=[anywhere] * 5, out_spe...  86.4 us
    pallas_call x1, Pallas kernels, shards(): pl.pallas_call(settle, out_shape=shapes, in_specs=[anywhere] * 4, out_spe...  3.28 us

profile of v4, /device:TPU:12, one launch (start us, length us, event | category | flops | bytes accessed | tf_op | source)
XLA Modules:
  0.0 90.3 jit_solution(10520187768516694354)
XLA Ops:
  0.6 86.4 %ring_attention.1 = (bf16[5120,128]{1,0:T(8,128)(2,1)}, bf16[5120,128]{1,0:T(8,128)(2,1)}, bf16[1024,128]{1,0:T(8,128)(2,1)}, bf16[1024,128]{1,0:T(8,128)(2,1)}) custom-call(bf16[5120,128]{1,0:T(8,128)(2,1)} %bitcast.9, bf16[5120,128]{1,0:T(8,128)(2,1)} %bitcast.10, bf16[1024,128]{1,0:T(8,128)(2,1)} %bitcast.11, bf16[1024,128]{1,0:T(8,128)(2,1)} %bitcast.12, ...), custom_call_target="tpu_custom_call" | custom-call | tf_op jit(solution)/shard_map/ring_attention/pallas_call | solution.py:443
  87.0 3.3 %settle.1 = (bf16[5120,128]{1,0:T(8,128)(2,1)}, bf16[5120,128]{1,0:T(8,128)(2,1)}, bf16[1024,128]{1,0:T(8,128)(2,1)}, bf16[1024,128]{1,0:T(8,128)(2,1)}) custom-call(bf16[5120,128]{1,0:T(8,128)(2,1)} %get-tuple-element.12.refs_0_, bf16[5120,128]{1,0:T(8,128)(2,1)} %get-tuple-element.13.refs_1_, bf16[1024,128]{1,0:T(8,128)(2,1)} %get-tuple-element.14.refs_2_, ...), custom_call_target="tpu_custom_call" | custom-call | tf_op jit(solution)/shard_map/settle/pallas_call | solution.py:493
